TPU v7x, 32 devices: a whole 2x2x4 slice. The times are simulated.
32 devices in a mesh: blk: 8 (over y, x, core), uly: 4 (over z).
Axes of the slice: x: 2, y: 2, z: 4, core: 2. Of those that a mesh axis runs over, the one named last changes fastest.
Arguments:
- tokens: bfloat16 [1536, 2048], P(('blk', 'uly')), may hold values from -6 to 6
- mod_shift: float32 [2048], replicated, may hold values from -3 to 3
- mod_scale: float32 [2048], replicated, may hold values from -2.5 to 2.5
- mod_gate: float32 [2048], replicated, may hold values from 0.25 to 1.5
- w_query: bfloat16 [2048, 2048], P(None, 'uly'), may hold values from -0.125 to 0.125
- w_key: bfloat16 [2048, 2048], P(None, 'uly'), may hold values from -0.125 to 0.125
- w_value: bfloat16 [2048, 2048], P(None, 'uly'), may hold values from -0.125 to 0.125
- w_out: bfloat16 [2048, 2048], P('uly'), may hold values from -0.125 to 0.125
- score_gain: float32 [32], replicated, may hold values from 4 to 40, as said below
Outputs:
- block_out: bfloat16 [1536, 2048], P(('blk', 'uly'))
Inputs may be any that keep to these rules, and one draw needn't show every extreme that they name: `score_gain`: one positive factor for each head.
All inputs are finite; a program needn't handle non-finite values.
Results may differ from a plain program's by a relative error of at most 0.012.
The roundings to bfloat16 on the way count: a program that leaves them out, or rounds other values in their place, can miss the bound.
Values may be sent and summed in bfloat16 or wider, within the bound.
A program may use at most 192 MiB of HBM per device.

v0:
```python
import math

import jax
import jax.numpy as jnp
from jax import lax
from jax.sharding import PartitionSpec as P

D = 2048
HEADS = 32


def modulate(tokens, mod_shift, mod_scale):
    values = tokens.astype(jnp.float32)
    center = values - jnp.mean(values, axis=-1, keepdims=True)
    spread = jnp.mean(center * center, axis=-1, keepdims=True)
    normed = center * lax.rsqrt(spread + 1e-06)
    return (normed * (1.0 + mod_scale) + mod_shift).astype(jnp.bfloat16)


def head_norm(projected, width):
    count = projected.shape[0]
    split = projected.reshape(count, -1, width)
    power = jnp.mean(split * split, axis=-1, keepdims=True)
    return (split * lax.rsqrt(power + 1e-06)).reshape(count, -1).astype(jnp.bfloat16)


def body(tokens, mod_shift, mod_scale, mod_gate, w_query, w_key, w_value, w_out, score_gain):
    width = D // HEADS
    local_cols = w_query.shape[1]
    local_heads = local_cols // width
    modded = modulate(tokens, mod_shift, mod_scale)
    piece = lax.all_gather(modded, "uly", axis=0, tiled=True)
    joined = jnp.concatenate(
        [
            jnp.dot(piece, w_query, preferred_element_type=jnp.float32),
            jnp.dot(piece, w_key, preferred_element_type=jnp.float32),
            jnp.dot(piece, w_value, preferred_element_type=jnp.float32),
        ],
        axis=1,
    )
    queries = head_norm(joined[:, :local_cols], width)
    keys = head_norm(joined[:, local_cols : 2 * local_cols], width)
    values = joined[:, 2 * local_cols :].astype(jnp.bfloat16)
    gains = lax.dynamic_slice_in_dim(score_gain, lax.axis_index("uly") * local_heads, local_heads)
    factors = gains / math.sqrt(width)
    rows = queries.shape[0]
    query_heads = queries.reshape(rows, local_heads, width)
    initial = (
        jnp.full((local_heads, rows), -jnp.inf, jnp.float32),
        jnp.zeros((local_heads, rows), jnp.float32),
        jnp.zeros((local_heads, rows, width), jnp.float32),
    )
    key_piece = lax.all_gather(keys, "blk", axis=0, tiled=True)
    value_piece = lax.all_gather(values, "blk", axis=0, tiled=True)
    count = key_piece.shape[0]
    groups = count // rows
    limit = max(rows, 1024)
    depth = max(
        [step for step in range(1, groups + 1) if groups % step == 0 and step * rows <= limit]
    )
    stride = depth * rows
    key_blocks = key_piece.reshape(count // stride, stride, local_heads, width)
    value_blocks = value_piece.reshape(count // stride, stride, local_heads, width)

    def one_block(carry, blocks):
        run_max, run_total, run_acc = carry
        key_block, value_block = blocks
        scores = jnp.einsum(
            "rhd,khd->hrk", query_heads, key_block, preferred_element_type=jnp.float32
        )
        scores = scores * factors[:, None, None]
        new_max = jnp.maximum(run_max, jnp.max(scores, axis=-1))
        expo = jnp.exp(scores - new_max[..., None])
        rescale = jnp.exp(run_max - new_max)
        new_total = run_total * rescale + jnp.sum(expo, axis=-1)
        summed = jnp.einsum(
            "hrk,khd->hrd",
            expo.astype(jnp.bfloat16),
            value_block,
            preferred_element_type=jnp.float32,
        )
        new_acc = run_acc * rescale[..., None] + summed
        return ((new_max, new_total, new_acc), None)

    result, unused = lax.scan(one_block, initial, (key_blocks, value_blocks))
    run_max, run_total, run_acc = result
    attended = (run_acc / run_total[..., None]).astype(jnp.bfloat16)
    attended = attended.transpose(1, 0, 2).reshape(rows, local_cols)
    returned = lax.all_to_all(attended, "uly", split_axis=0, concat_axis=1, tiled=True)
    projected = jnp.dot(
        returned,
        lax.all_gather(w_out, "uly", axis=0, tiled=True),
        preferred_element_type=jnp.float32,
    )
    return (tokens.astype(jnp.float32) + mod_gate * projected).astype(jnp.bfloat16)


def solution(mesh):
    in_specs = (
        P(("blk", "uly"), None),
        P(),
        P(),
        P(),
        P(None, "uly"),
        P(None, "uly"),
        P(None, "uly"),
        P("uly", None),
        P(),
    )
    out_specs = P(("blk", "uly"), None)
    return jax.shard_map(body, mesh=mesh, in_specs=in_specs, out_specs=out_specs, check_vma=False)
```

profile of v0, /device:TPU:0, one launch (start us, length us, event | category | flops | bytes accessed | tf_op | source)
XLA Modules:
  0.0 258.0 jit_solution(16467497553969542075)
XLA Ops:
  6.5 0.0 copy-start
  6.5 0.0 all-gather.4.cloned.1.call-start
  6.5 1.2 convert_reduce_fusion
  7.8 1.2 fusion.22
  8.9 0.7 broadcast_add_fusion
  9.6 1.1 fusion.25
  10.7 21.3 %all_gather.12 = bf16[192,2048]{1,0:T(8,128)(2,1)S(1)} all-gather(bf16[48,2048]{1,0:T(8,128)(2,1)S(1)} %fusion.25), channel_id=1, replica_groups=mesh['blk'=8,'uly'=4] {'uly'}, dimensions={0}, use_global_device_ids=true | all-gather | bytes 983040 | tf_op jit(solution)/shard_map/all_gather | solution.py:32
  32.0 0.0 copy-done
  32.0 1.5 fusion.27
  33.5 1.2 copy.13
  34.7 0.1 bitcast_reduce_fusion.2
  34.8 0.9 copy.14
  35.7 1.8 multiply_convert_fusion.1
  37.5 0.0 all-gather.4.cloned.1.call-update
  37.6 0.0 all-gather.6.cloned.1.call-start
  37.6 2.8 %convolution_convert_fusion = bf16[192,512]{1,0:T(8,128)(2,1)} fusion(bf16[192,2048]{1,0:T(8,128)(2,1)S(1)} %all_gather.12, bf16[2048,512]{1,0:T(8,128)(2,1)} %param.17), kind=kOutput, calls=%fused_computation.24 | convolution fusion | flops 402751488 | bytes 3080192 | tf_op jit(solution)/shard_map/dot_general | solution.py:37
  40.5 0.0 all-gather.6.cloned.1.call-update
  40.5 0.0 all-gather.8.cloned.1.call-start
  40.5 0.7 all-gather.8.cloned.1.call-update
  41.3 3.1 %fusion.28 = (f32[192,512]{1,0:T(8,128)}, f32[192,512]{1,0:T(8,128)}) fusion(bf16[192,2048]{1,0:T(8,128)(2,1)S(1)} %all_gather.12, bf16[2048,512]{1,0:T(8,128)(2,1)} %param.15), kind=kOutput, calls=%fused_computation.46 | convolution fusion | flops 402751488 | bytes 3670016 | tf_op jit(solution)/shard_map/dot_general | solution.py:35
  44.4 1.3 copy.16
  45.6 0.1 bitcast_reduce_fusion.1
  45.8 1.0 copy.17
  46.7 1.0 multiply_convert_fusion
  47.8 0.1 copy.18
  47.9 0.7 dynamic-slice_multiply_fusion
  48.7 14.1 %all-gather.4.cloned.1.call-done = bf16[1536,512]{1,0:T(8,128)(2,1)} async-done(((bf16[192,512]{1,0:T(8,128)(2,1)}), bf16[1536,512]{1,0:T(8,128)(2,1)}) %all-gather.4.cloned.1.call-update) | async-done | bytes 1572880 | tf_op jit(solution)/shard_map/all_gather | solution.py:53
  62.8 5.1 %reshape.60 = bf16[2,768,8,64]{3,2,1,0:T(8,128)(2,1)} reshape(bf16[1536,512]{1,0:T(8,128)(2,1)} %all-gather.4.cloned.1.call-done) | data formatting | bytes 3145728 | tf_op jit(solution)/shard_map/reshape | solution.py:62
  67.9 4.4 %copy.20 = bf16[2,768,8,64]{1,3,2,0:T(8,128)(2,1)} copy(bf16[2,768,8,64]{3,2,1,0:T(8,128)(2,1)} %reshape.60) | data formatting | bytes 3145728
  72.3 18.0 %all-gather.6.cloned.1.call-done = bf16[1536,512]{1,0:T(8,128)(2,1)} async-done(((bf16[192,512]{1,0:T(8,128)(2,1)}), bf16[1536,512]{1,0:T(8,128)(2,1)}) %all-gather.6.cloned.1.call-update) | async-done | bytes 1572880 | tf_op jit(solution)/shard_map/all_gather | solution.py:54
  90.4 5.1 %reshape.61 = bf16[2,768,8,64]{3,2,1,0:T(8,128)(2,1)} reshape(bf16[1536,512]{1,0:T(8,128)(2,1)} %all-gather.6.cloned.1.call-done) | data formatting | bytes 3145728 | tf_op jit(solution)/shard_map/reshape | solution.py:63
  95.5 4.7 %copy.21 = bf16[2,768,8,64]{1,3,2,0:T(8,128)(2,1)} copy(bf16[2,768,8,64]{3,2,1,0:T(8,128)(2,1)} %reshape.61) | data formatting | bytes 3145728
  100.2 20.8 %while.15 = (s32[]{:T(128)}, f32[8,192]{1,0:T(8,128)S(1)}, f32[8,192]{1,0:T(8,128)S(1)}, f32[8,192,64]{1,2,0:T(8,128)S(1)}, bf16[2,768,8,64]{1,3,2,0:T(8,128)(2,...) while((s32[]{:T(128)}, f32[8,192]{1,0:T(8,128)S(1)}, ...), condition=%wide.region_7.8_spmd.clone, body=%wide.region_4.7_spmd.clone.sunk | while | flops 311729664 | bytes 35685612 | solution.py:85
  100.2 4.3 %bitcast_reduce_fusion.4 = (f32[8,192]{1,0:T(8,128)S(1)}, f32[8,768,192]{1,2,0:T(8,128)}) fusion(f32[8]{0:T(128)S(1)} %get-tuple-element.200, bf16[192,8,64]{0,2,1:T(8,128)(2,1)S(1)} %get-tuple-element.199, bf16[2,768,8,64]{1,3,2,0:T(8,128)(2,1)} %get-tuple-element.198, s32[]{:T(128)} %get-tuple-element.184), kind=kOutput, calls=%fused_computation.1.clone.1 | convolution fusion | flops 153352704 | bytes 5708320 | tf_op jit(solution)/shard_map/while/body/eval_jaxpr/rhd,khd->hrk/dot_general | solution.py:68
  104.5 3.7 %fusion.47 = f32[8,192]{1,0:T(8,128)S(1)} fusion(f32[8,768,192]{1,2,0:T(8,128)} %get-tuple-element.171, f32[8,192]{1,0:T(8,128)S(1)} %select_maximum_fusion.2, f32[8]{0:T(128)S(1)} %get-tuple-element.200), kind=kLoop, calls=%fused_computation.4.clone.1 | loop fusion | flops 3537408 | bytes 4730912 | tf_op jit(solution)/shard_map/while/body/eval_jaxpr/reduce_sum | solution.py:75
  108.3 0.2 copy-done.1
  108.4 2.3 fusion.49
  110.8 4.1 %bitcast_reduce_fusion.4 = (f32[8,192]{1,0:T(8,128)S(1)}, f32[8,768,192]{1,2,0:T(8,128)}) fusion(f32[8]{0:T(128)S(1)} %get-tuple-element.200, bf16[192,8,64]{0,2,1:T(8,128)(2,1)S(1)} %get-tuple-element.199, bf16[2,768,8,64]{1,3,2,0:T(8,128)(2,1)} %get-tuple-element.198, s32[]{:T(128)} %get-tuple-element.184), kind=kOutput, calls=%fused_computation.1.clone.1 | convolution fusion | flops 153352704 | bytes 5708320 | tf_op jit(solution)/shard_map/while/body/eval_jaxpr/rhd,khd->hrk/dot_general | solution.py:68
  114.9 3.6 %fusion.47 = f32[8,192]{1,0:T(8,128)S(1)} fusion(f32[8,768,192]{1,2,0:T(8,128)} %get-tuple-element.171, f32[8,192]{1,0:T(8,128)S(1)} %select_maximum_fusion.2, f32[8]{0:T(128)S(1)} %get-tuple-element.200), kind=kLoop, calls=%fused_computation.4.clone.1 | loop fusion | flops 3537408 | bytes 4730912 | tf_op jit(solution)/shard_map/while/body/eval_jaxpr/reduce_sum | solution.py:75
  118.5 0.1 copy-done.1
  118.7 2.3 fusion.49
  121.0 0.1 fusion.26
  121.1 0.2 copy.22
  121.3 0.3 all_to_all.14
  121.6 19.0 %all_to_all.19 = bf16[4,48,512]{2,1,0:T(8,128)(2,1)S(1)} all-to-all(bf16[4,48,512]{2,1,0:T(8,128)(2,1)S(1)} %all_to_all.14), channel_id=1, replica_groups=mesh['blk'=8,'uly'=4] {'uly'}, dimensions={0} | all-to-all | bytes 393216 | tf_op jit(solution)/shard_map/all_to_all | solution.py:89
  140.6 105.2 %all-gather.8.cloned.1.call-done = bf16[2048,2048]{1,0:T(8,128)(2,1)} async-done(((bf16[512,2048]{1,0:T(8,128)(2,1)}), bf16[2048,2048]{1,0:T(8,128)(2,1)}) %all-gather.8.cloned.1.call-update) | async-done | bytes 8388624 | tf_op jit(solution)/shard_map/all_gather | solution.py:92
  245.8 0.0 copy-done.4
  245.8 5.6 %fusion.19 = bf16[48,2048]{1,0:T(8,128)(2,1)} fusion(bf16[48,2048]{1,0:T(8,128)(2,1)S(1)} %bitcast.56, bf16[2048,2048]{1,0:T(8,128)(2,1)} %all-gather.8.cloned.1.call-done, bf16[48,2048]{1,0:T(8,128)(2,1)S(1)} %copy-done.2, f32[2048]{0:T(1024)S(1)} %copy-done.4), kind=kOutput, calls=%fused_computation.23 | convolution fusion | flops 403046400 | bytes 8986624 | tf_op jit(solution)/shard_map/dot_general | solution.py:90
  (23 shorter events, 0.2 us)
Async XLA Ops:
  6.5 25.5 %copy-start = (bf16[2048,512]{1,0:T(8,128)(2,1)S(1)}, bf16[2048,512]{1,0:T(8,128)(2,1)}, u32[]{:S(2)}) copy-start(bf16[2048,512]{1,0:T(8,128)(2,1)} %param.16) | copy-start | bytes 6291460
  6.5 56.2 %all-gather.4.cloned.1.call-start = ((), (), s32[]{:S(2)}) async-start(), calls=%async_computation.1 | async-start | bytes 1769472 | tf_op jit(solution)/shard_map/all_gather | solution.py:53
  37.6 52.8 %all-gather.6.cloned.1.call-start = ((), (), s32[]{:S(2)}) async-start(), calls=%async_computation.2 | async-start | bytes 1769472 | tf_op jit(solution)/shard_map/all_gather | solution.py:54
  40.5 205.3 %all-gather.8.cloned.1.call-start = ((), (), s32[]{:S(2)}) async-start(), calls=%async_computation.3 | async-start | bytes 10485760 | tf_op jit(solution)/shard_map/all_gather | solution.py:92
  44.4 2.4 copy-start.3
  100.2 145.6 %copy-start.2 = (bf16[48,2048]{1,0:T(8,128)(2,1)S(1)}, bf16[48,2048]{1,0:T(8,128)(2,1)}, u32[]{:S(2)}) copy-start(bf16[48,2048]{1,0:T(8,128)(2,1)} %param.11) | copy-start | bytes 589828
  100.2 145.6 %copy-start.4 = (f32[2048]{0:T(1024)S(1)}, f32[2048]{0:T(1024)}, u32[]{:S(2)}) copy-start(f32[2048]{0:T(1024)} %param.14) | copy-start | bytes 24580
  104.5 3.9 %copy-start.1 = (f32[8,768,192]{1,2,0:T(8,128)S(1)}, f32[8,768,192]{1,2,0:T(8,128)}, u32[]{:S(2)}) copy-start(f32[8,768,192]{1,2,0:T(8,128)} %get-tuple-element.171) | copy-start | bytes 14155780 | tf_op jit(solution)/shard_map/while
  114.9 3.8 %copy-start.1 = (f32[8,768,192]{1,2,0:T(8,128)S(1)}, f32[8,768,192]{1,2,0:T(8,128)}, u32[]{:S(2)}) copy-start(f32[8,768,192]{1,2,0:T(8,128)} %get-tuple-element.171) | copy-start | bytes 14155780 | tf_op jit(solution)/shard_map/while
Sparse Core Ops, SparseCore 0:
  37.7 25.0 all-gather.3
  64.6 25.6 all-gather.5
  91.9 153.7 all-gather.7
where the time goes:
time: 259 us; the launch traced here: 258 us
  waiting for transfers between devices  138 us (53%)
  blocking collectives  40.3 us (16%)
  matrix products  26.1 us (10%)
  local copies, waits for them, and re-layouts  24.8 us (10%)
  other arithmetic  15.3 us (6%)
  between operations  13.3 us (5%)
    all_gather x1, waiting for transfers between devices, body(): lax.all_gather(w_out, 'uly', axis=0, tiled=True)  105 us
    all_gather x1, blocking collectives, body(): piece = lax.all_gather(modded, 'uly', axis=0, tiled=True)  21.3 us
    all_to_all x1, blocking collectives, body(): lax.all_to_all(attended, 'uly', split_axis=0, concat_axis=1, tiled=True)  19 us
    all_gather x1, waiting for transfers between devices, body(): value_piece = lax.all_gather(values, 'blk', axis=0, tiled=True)  18 us
    all_gather x1, waiting for transfers between devices, body(): key_piece = lax.all_gather(keys, 'blk', axis=0, tiled=True)  14.1 us
    unnamed x10, local copies, waits for them, and re-layouts  9.16 us
    dot_general x2, matrix products, one_block(): jnp.einsum('rhd,khd->hrk', query_heads, key_block, preferred_element_type...  8.44 us
    reduce_sum x2, other arithmetic, one_block(): new_total = run_total * rescale + jnp.sum(expo, axis=-1)  7.34 us
  transfers between devices with their start and end apart: 3, of which 3 were waited for; matrix products, arithmetic and copies ran while one was open for 20% of the time, Pallas kernels for 0%

commit v1 on v0

--- a/solution.py
+++ b/solution.py
@@ -1,12 +1,257 @@
+import functools
 import math
 
 import jax
 import jax.numpy as jnp
 from jax import lax
+from jax.experimental import pallas as pl
+from jax.experimental.pallas import tpu as pltpu
 from jax.sharding import PartitionSpec as P
 
 D = 2048
 HEADS = 32
+LOG2E = math.log2(math.e)
+MESH = pl.DeviceIdType.MESH
+
+
+def kernel(
+    nb, nz, tok, shift, scale, gate, gain, wq, wk, wv, wo, out,
+    mod, wq_v, wk_v, wv_v, wo_v, snd, rcv, asnd, arcv, own, rsnd, rrcv,
+    wsem, gs, gr, hs, hr, bs, br, rs, rr,
+):
+    width = D // HEADS
+    rows = tok.shape[0]
+    block = nz * rows
+    half = block // 2
+    tile = rrcv.shape[-1]
+    parts = D // tile
+    mb, mz = lax.axis_index("blk"), lax.axis_index("uly")
+
+    loads = [
+        pltpu.make_async_copy(src, dst, wsem.at[i])
+        for i, (src, dst) in enumerate(((wq, wq_v), (wk, wk_v), (wv, wv_v), (wo, wo_v)))
+    ]
+    for load in loads:
+        load.start()
+
+    barrier = pltpu.get_barrier_semaphore()
+    for j in range(1, nz):
+        pl.semaphore_signal(barrier, inc=1, device_id={"uly": lax.rem(mz + j, nz)}, device_id_type=MESH)
+    for j in range(1, nb):
+        pl.semaphore_signal(barrier, inc=1, device_id={"blk": lax.rem(mb + j, nb)}, device_id_type=MESH)
+
+    def order(k):
+        if nz != 4:
+            return lax.rem(mz + k, nz)
+        high = mz // 2
+        near = mz + 1 - 2 * lax.rem(mz, 2)
+        return jnp.where(k == 0, mz, jnp.where(k == 1, near, jnp.where(k == 2, 2 - high, 3 - 3 * high)))
+
+    values = tok[...].astype(jnp.float32)
+    center = values - jnp.mean(values, axis=-1, keepdims=True)
+    spread = jnp.mean(center * center, axis=-1, keepdims=True)
+    normed = center * lax.rsqrt(spread + 1e-06)
+    mod[mz] = (normed * (1.0 + scale[...]) + shift[...]).astype(jnp.bfloat16)
+
+    pl.semaphore_wait(barrier, nz - 1 + nb - 1)
+
+    def gather(z):
+        return pltpu.make_async_remote_copy(
+            src_ref=mod.at[mz], dst_ref=mod.at[mz], send_sem=gs.at[z], recv_sem=gr.at[mz],
+            device_id={"uly": z}, device_id_type=MESH)
+
+    def gathered(z):
+        return pltpu.make_async_remote_copy(
+            src_ref=mod.at[z], dst_ref=mod.at[z], send_sem=gs.at[z], recv_sem=gr.at[z],
+            device_id={"uly": z}, device_id_type=MESH)
+
+    for k in range(nz - 1, 0, -1):
+        gather(order(k)).start()
+    for load in loads[:3]:
+        load.wait()
+
+    def spot(b, z):
+        return pl.ds(pl.multiple_of((b * nz + z) * rows, rows), rows)
+
+    def heads_to(z, b):
+        return pltpu.make_async_remote_copy(
+            src_ref=snd.at[z, b], dst_ref=rcv.at[:, spot(mb, z), :], send_sem=hs.at[z, b],
+            recv_sem=hr.at[z, mb], device_id={"blk": b}, device_id_type=MESH)
+
+    def heads_from(z, b):
+        return pltpu.make_async_remote_copy(
+            src_ref=snd.at[z, b], dst_ref=rcv.at[:, spot(b, z), :], send_sem=hs.at[z, b],
+            recv_sem=hr.at[z, b], device_id={"blk": b}, device_id_type=MESH)
+
+    def piece(k, carry):
+        z = order(k)
+
+        @pl.when(k > 0)
+        def _():
+            gathered(z).wait_recv()
+
+        x = mod[z]
+        query = jnp.dot(x, wq_v[...], preferred_element_type=jnp.float32)
+        key = jnp.dot(x, wk_v[...], preferred_element_type=jnp.float32)
+        value = jnp.dot(x, wv_v[...], preferred_element_type=jnp.float32)
+
+        def unit(part):
+            power = jnp.mean(part * part, axis=-1, keepdims=True)
+            return part * lax.rsqrt(power + 1e-06)
+
+        for h in range(nb):
+            cols = slice(h * width, (h + 1) * width)
+            snd[z, h, 0] = jnp.concatenate([unit(key[:, cols]), value[:, cols]], axis=1).astype(jnp.bfloat16)
+            line = unit(query[:, cols])
+            snd[z, h, 1] = jnp.concatenate([line, jnp.zeros_like(line)], axis=1).astype(jnp.bfloat16)
+        rcv[:, spot(mb, z), :] = snd[z, mb]
+
+        def send(j, carry):
+            heads_to(z, lax.rem(mb + j, nb)).start()
+            return carry
+
+        lax.fori_loop(1, nb, send, 0)
+        return carry
+
+    lax.fori_loop(0, nz, piece, 0)
+
+    def arrive(i, carry):
+        heads_from(order(i // (nb - 1)), lax.rem(mb + 1 + lax.rem(i, nb - 1), nb)).wait_recv()
+        return carry
+
+    lax.fori_loop(0, nz * (nb - 1), arrive, 0)
+
+    factor = gain[mz * nb + mb] * (LOG2E / math.sqrt(width))
+
+    def back_to(b):
+        return pltpu.make_async_remote_copy(
+            src_ref=asnd.at[b], dst_ref=arcv.at[mb], send_sem=bs.at[b], recv_sem=br.at[mb],
+            device_id={"blk": b}, device_id_type=MESH)
+
+    def back_from(b):
+        return pltpu.make_async_remote_copy(
+            src_ref=asnd.at[b], dst_ref=arcv.at[b], send_sem=bs.at[b], recv_sem=br.at[b],
+            device_id={"blk": b}, device_id_type=MESH)
+
+    def attend(k, carry):
+        b = lax.rem(mb + k, nb)
+        q = rcv[1, pl.ds(pl.multiple_of(b * block, block), block), :]
+        kv = rcv[0]
+        scores = lax.dot_general(q, kv, (((1,), (1,)), ((), ())), preferred_element_type=jnp.float32)
+        top = jnp.max(scores, axis=-1, keepdims=True)
+        expo = jnp.exp2((scores - top) * factor)
+        total = jnp.sum(expo, axis=-1, keepdims=True)
+        summed = jnp.dot(expo.astype(jnp.bfloat16), kv, preferred_element_type=jnp.float32) / total
+        packed = jnp.concatenate([summed[:half, width:], summed[half:, width:]], axis=1)
+        asnd[b] = packed.astype(jnp.bfloat16)
+
+        @pl.when(k < nb)
+        def _():
+            back_to(b).start()
+
+        return carry
+
+    lax.fori_loop(1, nb + 1, attend, 0)
+    arcv[mb] = asnd[mb]
+    loads[3].wait()
+    for j in range(1, nb):
+        back_from(lax.rem(mb + j, nb)).wait_recv()
+
+    pieces = [arcv[h] for h in range(nb)]
+    attended = jnp.concatenate(
+        [
+            jnp.concatenate([part[:, :width] for part in pieces], axis=1),
+            jnp.concatenate([part[:, width:] for part in pieces], axis=1),
+        ],
+        axis=0,
+    )
+
+    def sum_to(n, z):
+        return pltpu.make_async_remote_copy(
+            src_ref=rsnd.at[n, z], dst_ref=rrcv.at[n, mz], send_sem=rs.at[n, z], recv_sem=rr.at[n, mz],
+            device_id={"uly": z}, device_id_type=MESH)
+
+    def sum_from(n, z):
+        return pltpu.make_async_remote_copy(
+            src_ref=rsnd.at[n, z], dst_ref=rrcv.at[n, z], send_sem=rs.at[n, z], recv_sem=rr.at[n, z],
+            device_id={"uly": z}, device_id_type=MESH)
+
+    for n in range(parts):
+        part = jnp.dot(attended, wo_v[:, n * tile : (n + 1) * tile], preferred_element_type=jnp.float32)
+        for z in range(nz):
+            own[n, z] = part[z * rows : (z + 1) * rows]
+            rsnd[n, z] = part[z * rows : (z + 1) * rows].astype(jnp.bfloat16)
+        for k in range(nz - 1, 0, -1):
+            sum_to(n, order(k)).start()
+    for n in range(parts):
+        total = own[n, mz]
+        for k in range(1, nz):
+            z = order(k)
+            sum_from(n, z).wait_recv()
+            total = total + rrcv[n, z].astype(jnp.float32)
+        cols = slice(n * tile, (n + 1) * tile)
+        out[:, cols] = (tok[:, cols].astype(jnp.float32) + gate[:, cols] * total).astype(jnp.bfloat16)
+
+    for k in range(1, nz):
+        gather(order(k)).wait_send()
+
+    def sent(i, carry):
+        heads_to(order(i // (nb - 1)), lax.rem(mb + 1 + lax.rem(i, nb - 1), nb)).wait_send()
+        return carry
+
+    lax.fori_loop(0, nz * (nb - 1), sent, 0)
+    for j in range(1, nb):
+        back_to(lax.rem(mb + j, nb)).wait_send()
+    for n in range(parts):
+        for k in range(1, nz):
+            sum_to(n, order(k)).wait_send()
+
+
+def fused(nb, nz, tokens, mod_shift, mod_scale, mod_gate, w_query, w_key, w_value, w_out, score_gain):
+    rows = tokens.shape[0]
+    cols = w_query.shape[1]
+    tile = 512
+    parts = D // tile
+    bf16, f32 = jnp.bfloat16, jnp.float32
+    vmem = pl.BlockSpec(memory_space=pltpu.VMEM)
+    smem = pl.BlockSpec(memory_space=pltpu.SMEM)
+    anywhere = pl.BlockSpec(memory_space=pl.ANY)
+    dma = pltpu.SemaphoreType.DMA
+    return pl.pallas_call(
+        functools.partial(kernel, nb, nz),
+        out_shape=jax.ShapeDtypeStruct((rows, D), bf16),
+        in_specs=[vmem] * 4 + [smem] + [anywhere] * 4,
+        out_specs=vmem,
+        scratch_shapes=[
+            pltpu.VMEM((nz, rows, D), bf16),
+            pltpu.VMEM((D, cols), bf16),
+            pltpu.VMEM((D, cols), bf16),
+            pltpu.VMEM((D, cols), bf16),
+            pltpu.VMEM((cols, D), bf16),
+            pltpu.VMEM((nz, nb, 2, rows, 128), bf16),
+            pltpu.VMEM((2, nb * nz * rows, 128), bf16),
+            pltpu.VMEM((nb, nz * rows // 2, 128), bf16),
+            pltpu.VMEM((nb, nz * rows // 2, 128), bf16),
+            pltpu.VMEM((parts, nz, rows, tile), f32),
+            pltpu.VMEM((parts, nz, rows, tile), bf16),
+            pltpu.VMEM((parts, nz, rows, tile), bf16),
+            dma((4,)),
+            dma((nz,)),
+            dma((nz,)),
+            dma((nz, nb)),
+            dma((nz, nb)),
+            dma((nb,)),
+            dma((nb,)),
+            dma((parts, nz)),
+            dma((parts, nz)),
+        ],
+        compiler_params=pltpu.CompilerParams(
+            collective_id=0, has_side_effects=True, vmem_limit_bytes=40 * 1024 * 1024
+        ),
+    )(
+        tokens, mod_shift[None], mod_scale[None], mod_gate[None], score_gain,
+        w_query, w_key, w_value, w_out,
+    )
 
 
 def modulate(tokens, mod_shift, mod_scale):
@@ -108,4 +353,8 @@
         P(),
     )
     out_specs = P(("blk", "uly"), None)
-    return jax.shard_map(body, mesh=mesh, in_specs=in_specs, out_specs=out_specs, check_vma=False)
+    nb, nz = mesh.shape["blk"], mesh.shape["uly"]
+    run = body
+    if HEADS == nb * nz:
+        run = functools.partial(fused, nb, nz)
+    return jax.shard_map(run, mesh=mesh, in_specs=in_specs, out_specs=out_specs, check_vma=False)

time: 259 us -> 69.3 us (0.27)
  waiting for transfers between devices: 138 us -> 0 us
  Pallas kernels: 0 us -> 58.2 us
  blocking collectives: 40.3 us -> 0 us
  matrix products: 26.1 us -> 0 us
  other arithmetic: 15.3 us -> 0 us
  local copies, waits for them, and re-layouts: 24.8 us -> 10.7 us
  between operations: 13.3 us -> 0.02 us
    all_gather x3 -> x0, waiting for transfers between devices: 137 us -> none  [the longest x1 105 us: body(): lax.all_gather(w_out, 'uly', axis=0, tiled=True)]
    pallas_call x0 -> x1, Pallas kernels: none -> 58.2 us  [fused(): pl.pallas_call(functools.partial(kernel, nb, nz), out_shape=jax.ShapeDtyp...]
    dot_general x8 -> x0, matrix products: 26.1 us -> none  [the longest x2 8.44 us: one_block(): jnp.einsum('rhd,khd->hrk', query_heads, key_block, preferred_element_type...]
    all_gather x1 -> x0, blocking collectives: 21.3 us -> none  [body(): piece = lax.all_gather(modded, 'uly', axis=0, tiled=True)]
    all_to_all x1 -> x0, blocking collectives: 19 us -> none  [body(): lax.all_to_all(attended, 'uly', split_axis=0, concat_axis=1, tiled=True)]
    reshape x2 -> x0, local copies, waits for them, and re-layouts: 10.2 us -> none  [the longest x1 5.12 us: body(): key_blocks = key_piece.reshape(count // stride, stride, local_heads, width)]
    reduce_sum x6 -> x0, other arithmetic: 9.8 us -> none  [the longest x2 7.34 us: one_block(): new_total = run_total * rescale + jnp.sum(expo, axis=-1)]
    mul x6 -> x0, local copies, waits for them, and re-layouts: 4.43 us -> none  [the longest x2 2.46 us: head_norm(): power = jnp.mean(split * split, axis=-1, keepdims=True)]
  transfers between devices with their start and end apart: 3 -> 0, of which waited for: 3 -> 0; matrix products, arithmetic and copies ran while one was open for 20% -> 0% of each run, Pallas kernels for 0% -> 0%
where the time goes in v1:
time: 69.3 us; the launch traced here: 68.9 us
  Pallas kernels  58.2 us (84%)
  local copies, waits for them, and re-layouts  10.7 us (15%)
    pallas_call x1, Pallas kernels, fused(): pl.pallas_call(functools.partial(kernel, nb, nz), out_shape=jax.ShapeDtyp...  58.2 us
    unnamed x19, local copies, waits for them, and re-layouts  10.7 us

profile of v1, /device:TPU:0, one launch (start us, length us, event | category | flops | bytes accessed | tf_op | source)
XLA Modules:
  0.0 68.9 jit_solution(839762165421178797)
XLA Ops:
  0.0 0.0 copy-start
  0.0 1.6 %copy-done = bf16[2048,512]{1,0:T(8,128)(2,1)S(1)} copy-done((bf16[2048,512]{1,0:T(8,128)(2,1)S(1)}, bf16[2048,512]{1,0:T(8,128)(2,1)}, u32[]{:S(2)}) %copy-start) | copy-done | bytes 2097176
  1.6 0.0 copy-start.1
  1.6 1.6 %copy-done.1 = bf16[2048,512]{1,0:T(8,128)(2,1)S(1)} copy-done((bf16[2048,512]{1,0:T(8,128)(2,1)S(1)}, bf16[2048,512]{1,0:T(8,128)(2,1)}, u32[]{:S(2)}) %copy-start.1) | copy-done | bytes 2097176
  3.2 0.0 copy-start.2
  3.2 1.6 %copy-done.2 = bf16[2048,512]{1,0:T(8,128)(2,1)S(1)} copy-done((bf16[2048,512]{1,0:T(8,128)(2,1)S(1)}, bf16[2048,512]{1,0:T(8,128)(2,1)}, u32[]{:S(2)}) %copy-start.2) | copy-done | bytes 2097176
  4.8 0.0 copy-start.3
  4.8 1.6 %copy-done.3 = bf16[512,2048]{1,0:T(8,128)(2,1)S(1)} copy-done((bf16[512,2048]{1,0:T(8,128)(2,1)S(1)}, bf16[512,2048]{1,0:T(8,128)(2,1)}, u32[]{:S(2)}) %copy-start.3) | copy-done | bytes 2097176
  6.4 0.0 copy-start.4
  6.4 0.9 %copy-done.4 = bf16[48,2048]{1,0:T(8,128)(2,1)S(1)} copy-done((bf16[48,2048]{1,0:T(8,128)(2,1)S(1)}, bf16[48,2048]{1,0:T(8,128)(2,1)}, u32[]{:S(2)}) %copy-start.4) | copy-done | bytes 196632
  7.3 0.0 copy-start.5
  7.3 0.7 %copy-done.5 = f32[2048]{0:T(1024)S(1)} copy-done((f32[2048]{0:T(1024)S(1)}, f32[2048]{0:T(1024)}, u32[]{:S(2)}) %copy-start.5) | copy-done | bytes 8216
  8.0 0.0 copy-start.6
  8.0 0.7 %copy-done.6 = f32[2048]{0:T(1024)S(1)} copy-done((f32[2048]{0:T(1024)S(1)}, f32[2048]{0:T(1024)}, u32[]{:S(2)}) %copy-start.6) | copy-done | bytes 8216
  8.7 0.0 copy-start.7
  8.7 0.7 %copy-done.7 = f32[2048]{0:T(1024)S(1)} copy-done((f32[2048]{0:T(1024)S(1)}, f32[2048]{0:T(1024)}, u32[]{:S(2)}) %copy-start.7) | copy-done | bytes 8216
  9.4 0.0 copy-start.8
  9.4 0.7 copy-done.8
  10.0 58.2 %shard_map.91 = bf16[48,2048]{1,0:T(8,128)(2,1)S(1)} custom-call(bf16[48,2048]{1,0:T(8,128)(2,1)S(1)} %copy-done.4, f32[1,2048]{1,0:T(1,128)S(1)} %bitcast.3, f32[1,2048]{1,0:T(1,128)S(1)} %bitcast.4, f32[1,2048]{1,0:T(1,128)S(1)} %bitcast.5, f32[32]{0:T(128)S(1)} %copy-done.8, bf16[2048,512]{1,0:T(8,128)(2,1)S(1)} %copy-done, ...), custom_call_target="tpu_custom_call" | custom-call | tf_op jit(solution)/shard_map/pallas_call | solution.py:220
  68.2 0.7 copy.11
Async XLA Ops:
  0.0 1.6 %copy-start = (bf16[2048,512]{1,0:T(8,128)(2,1)S(1)}, bf16[2048,512]{1,0:T(8,128)(2,1)}, u32[]{:S(2)}) copy-start(bf16[2048,512]{1,0:T(8,128)(2,1)} %wq.1) | copy-start | bytes 6291460
  1.6 1.6 %copy-start.1 = (bf16[2048,512]{1,0:T(8,128)(2,1)S(1)}, bf16[2048,512]{1,0:T(8,128)(2,1)}, u32[]{:S(2)}) copy-start(bf16[2048,512]{1,0:T(8,128)(2,1)} %wk.1) | copy-start | bytes 6291460
  3.2 1.6 %copy-start.2 = (bf16[2048,512]{1,0:T(8,128)(2,1)S(1)}, bf16[2048,512]{1,0:T(8,128)(2,1)}, u32[]{:S(2)}) copy-start(bf16[2048,512]{1,0:T(8,128)(2,1)} %wv.1) | copy-start | bytes 6291460
  4.8 1.6 %copy-start.3 = (bf16[512,2048]{1,0:T(8,128)(2,1)S(1)}, bf16[512,2048]{1,0:T(8,128)(2,1)}, u32[]{:S(2)}) copy-start(bf16[512,2048]{1,0:T(8,128)(2,1)} %wo.1) | copy-start | bytes 6291460
  6.4 0.9 %copy-start.4 = (bf16[48,2048]{1,0:T(8,128)(2,1)S(1)}, bf16[48,2048]{1,0:T(8,128)(2,1)}, u32[]{:S(2)}) copy-start(bf16[48,2048]{1,0:T(8,128)(2,1)} %tok.1) | copy-start | bytes 589828
  7.3 0.7 %copy-start.5 = (f32[2048]{0:T(1024)S(1)}, f32[2048]{0:T(1024)}, u32[]{:S(2)}) copy-start(f32[2048]{0:T(1024)} %param.10) | copy-start | bytes 24580
  8.0 0.7 %copy-start.6 = (f32[2048]{0:T(1024)S(1)}, f32[2048]{0:T(1024)}, u32[]{:S(2)}) copy-start(f32[2048]{0:T(1024)} %param.11) | copy-start | bytes 24580
  8.7 0.7 %copy-start.7 = (f32[2048]{0:T(1024)S(1)}, f32[2048]{0:T(1024)}, u32[]{:S(2)}) copy-start(f32[2048]{0:T(1024)} %param.12) | copy-start | bytes 24580
  9.4 0.7 copy-start.8

commit v2 on v1

--- a/solution.py
+++ b/solution.py
@@ -15,9 +15,9 @@
 
 
 def kernel(
-    nb, nz, tok, shift, scale, gate, gain, wq, wk, wv, wo, out,
-    mod, wq_v, wk_v, wv_v, wo_v, snd, rcv, asnd, arcv, own, rsnd, rrcv,
-    wsem, gs, gr, hs, hr, bs, br, rs, rr,
+    nb, nz, tok_h, shift_h, scale_h, gate_h, gain_h, wq, wk, wv, wo, out,
+    tok, shift, scale, gate, gain, mod, wq_v, wk_v, wv_v, wo_v, snd, rcv, asnd, arcv, own, rsnd, rrcv,
+    wsem, gs, gr, fs, hs, hr, bs, br, rs, rr,
 ):
     width = D // HEADS
     rows = tok.shape[0]
@@ -27,9 +27,13 @@
     parts = D // tile
     mb, mz = lax.axis_index("blk"), lax.axis_index("uly")
 
+    pairs = (
+        (tok_h, tok), (shift_h, shift), (scale_h, scale), (wq, wq_v), (wk, wk_v), (wv, wv_v),
+        (wo, wo_v), (gate_h, gate), (gain_h, gain),
+    )
     loads = [
         pltpu.make_async_copy(src, dst, wsem.at[i])
-        for i, (src, dst) in enumerate(((wq, wq_v), (wk, wk_v), (wv, wv_v), (wo, wo_v)))
+        for i, (src, dst) in enumerate(pairs)
     ]
     for load in loads:
         load.start()
@@ -47,6 +51,12 @@
         near = mz + 1 - 2 * lax.rem(mz, 2)
         return jnp.where(k == 0, mz, jnp.where(k == 1, near, jnp.where(k == 2, 2 - high, 3 - 3 * high)))
 
+    for load in loads[:3]:
+        load.wait()
+    relayed = nz == 4
+    direct = (2, 1) if relayed else tuple(range(nz - 1, 0, -1))
+    middle = (mz + 1) // 2 == 1
+
     values = tok[...].astype(jnp.float32)
     center = values - jnp.mean(values, axis=-1, keepdims=True)
     spread = jnp.mean(center * center, axis=-1, keepdims=True)
@@ -65,9 +75,14 @@
             src_ref=mod.at[z], dst_ref=mod.at[z], send_sem=gs.at[z], recv_sem=gr.at[z],
             device_id={"uly": z}, device_id_type=MESH)
 
-    for k in range(nz - 1, 0, -1):
+    def forward(z):
+        return pltpu.make_async_remote_copy(
+            src_ref=mod.at[z], dst_ref=mod.at[z], send_sem=fs.at[z], recv_sem=gr.at[z],
+            device_id={"uly": order(1)}, device_id_type=MESH)
+
+    for k in direct:
         gather(order(k)).start()
-    for load in loads[:3]:
+    for load in loads[3:6]:
         load.wait()
 
     def spot(b, z):
@@ -89,6 +104,12 @@
         @pl.when(k > 0)
         def _():
             gathered(z).wait_recv()
+
+        if relayed:
+
+            @pl.when((k > 1) & middle)
+            def _():
+                forward(z).start()
 
         x = mod[z]
         query = jnp.dot(x, wq_v[...], preferred_element_type=jnp.float32)
@@ -121,7 +142,9 @@
 
     lax.fori_loop(0, nz * (nb - 1), arrive, 0)
 
-    factor = gain[mz * nb + mb] * (LOG2E / math.sqrt(width))
+    loads[8].wait()
+    chosen = lax.broadcasted_iota(jnp.int32, gain.shape, 1) == mz * nb + mb
+    factor = jnp.sum(jnp.where(chosen, gain[...], 0.0), axis=-1, keepdims=True) * (LOG2E / math.sqrt(width))
 
     def back_to(b):
         return pltpu.make_async_remote_copy(
@@ -153,7 +176,8 @@
 
     lax.fori_loop(1, nb + 1, attend, 0)
     arcv[mb] = asnd[mb]
-    loads[3].wait()
+    loads[6].wait()
+    loads[7].wait()
     for j in range(1, nb):
         back_from(lax.rem(mb + j, nb)).wait_recv()
 
@@ -192,8 +216,15 @@
         cols = slice(n * tile, (n + 1) * tile)
         out[:, cols] = (tok[:, cols].astype(jnp.float32) + gate[:, cols] * total).astype(jnp.bfloat16)
 
-    for k in range(1, nz):
+    for k in direct:
         gather(order(k)).wait_send()
+    if relayed:
+
+        @pl.when(middle)
+        def _():
+            for k in (2, 3):
+                forward(order(k)).wait_send()
+
 
     def sent(i, carry):
         heads_to(order(i // (nb - 1)), lax.rem(mb + 1 + lax.rem(i, nb - 1), nb)).wait_send()
@@ -214,15 +245,19 @@
     parts = D // tile
     bf16, f32 = jnp.bfloat16, jnp.float32
     vmem = pl.BlockSpec(memory_space=pltpu.VMEM)
-    smem = pl.BlockSpec(memory_space=pltpu.SMEM)
-    anywhere = pl.BlockSpec(memory_space=pl.ANY)
+    hbm = pl.BlockSpec(memory_space=pltpu.HBM)
     dma = pltpu.SemaphoreType.DMA
     return pl.pallas_call(
         functools.partial(kernel, nb, nz),
         out_shape=jax.ShapeDtypeStruct((rows, D), bf16),
-        in_specs=[vmem] * 4 + [smem] + [anywhere] * 4,
+        in_specs=[hbm] * 9,
         out_specs=vmem,
         scratch_shapes=[
+            pltpu.VMEM((rows, D), bf16),
+            pltpu.VMEM((1, D), f32),
+            pltpu.VMEM((1, D), f32),
+            pltpu.VMEM((1, D), f32),
+            pltpu.VMEM((1, HEADS), f32),
             pltpu.VMEM((nz, rows, D), bf16),
             pltpu.VMEM((D, cols), bf16),
             pltpu.VMEM((D, cols), bf16),
@@ -235,7 +270,8 @@
             pltpu.VMEM((parts, nz, rows, tile), f32),
             pltpu.VMEM((parts, nz, rows, tile), bf16),
             pltpu.VMEM((parts, nz, rows, tile), bf16),
-            dma((4,)),
+            dma((9,)),
+            dma((nz,)),
             dma((nz,)),
             dma((nz,)),
             dma((nz, nb)),
@@ -246,10 +282,10 @@
             dma((parts, nz)),
         ],
         compiler_params=pltpu.CompilerParams(
-            collective_id=0, has_side_effects=True, vmem_limit_bytes=40 * 1024 * 1024
+            collective_id=0, has_side_effects=True, vmem_limit_bytes=56 * 1024 * 1024
         ),
     )(
-        tokens, mod_shift[None], mod_scale[None], mod_gate[None], score_gain,
+        tokens, mod_shift[None], mod_scale[None], mod_gate[None], score_gain[None],
         w_query, w_key, w_value, w_out,
     )
 

time: 69.3 us -> 58.4 us (0.84)
  local copies, waits for them, and re-layouts: 10.7 us -> 1.62 us
  Pallas kernels: 58.2 us -> 56.6 us
    unnamed x19 -> x1, local copies, waits for them, and re-layouts: 10.7 us -> 1.62 us
    pallas_call x1, Pallas kernels: 58.2 us -> 56.6 us  [fused(): pl.pallas_call(functools.partial(kernel, nb, nz), out_shape=jax.ShapeDtyp...]
where the time goes in v2:
time: 58.4 us; the launch traced here: 58.3 us
  Pallas kernels  56.6 us (97%)
  local copies, waits for them, and re-layouts  1.62 us (3%)
    pallas_call x1, Pallas kernels, fused(): pl.pallas_call(functools.partial(kernel, nb, nz), out_shape=jax.ShapeDtyp...  56.6 us
    unnamed x1, local copies, waits for them, and re-layouts  1.62 us

profile of v2, /device:TPU:0, one launch (start us, length us, event | category | flops | bytes accessed | tf_op | source)
XLA Modules:
  0.0 58.3 jit_solution(14979119539424021510)
XLA Ops:
  0.0 56.6 %shard_map.91 = bf16[48,2048]{1,0:T(8,128)(2,1)} custom-call(bf16[48,2048]{1,0:T(8,128)(2,1)} %tok_h.1, f32[1,2048]{1,0:T(1,128)} %bitcast.4, f32[1,2048]{1,0:T(1,128)} %bitcast.5, f32[1,2048]{1,0:T(1,128)} %bitcast.6, f32[1,32]{1,0:T(1,128)} %bitcast.7, bf16[2048,512]{1,0:T(8,128)(2,1)} %wq.1, bf16[2048,512]{1,0:T(8,128)(2,1)} %wk.1, bf16[2048,512]{1,0:T(8,128)(2,1)} %wv.1, ...), custom_call_target="tpu_custom_call" | custom-call | tf_op jit(solution)/shard_map/pallas_call | solution.py:250
  56.6 1.6 %copy.11 = bf16[48,2048]{1,0:T(8,128)(2,1)} copy(bf16[48,2048]{1,0:T(8,128)(2,1)} %shard_map.91) | data formatting | bytes 393216

commit v3 on v2

--- a/solution.py
+++ b/solution.py
@@ -16,8 +16,8 @@
 
 def kernel(
     nb, nz, tok_h, shift_h, scale_h, gate_h, gain_h, wq, wk, wv, wo, out,
-    tok, shift, scale, gate, gain, mod, wq_v, wk_v, wv_v, wo_v, snd, rcv, asnd, arcv, own, rsnd, rrcv,
-    wsem, gs, gr, fs, hs, hr, bs, br, rs, rr,
+    tok, shift, scale, gate, gain, mod, wq_v, wk_v, wv_v, wo_v, snd, rcv, asnd, arcv, own, rsnd, rrcv, rel,
+    wsem, gs, gr, fs, hs, hr, bs, br, rs, rr, ls, lr,
 ):
     width = D // HEADS
     rows = tok.shape[0]
@@ -200,16 +200,40 @@
             src_ref=rsnd.at[n, z], dst_ref=rrcv.at[n, z], send_sem=rs.at[n, z], recv_sem=rr.at[n, z],
             device_id={"uly": z}, device_id_type=MESH)
 
+    def relay(n, z):
+        return pltpu.make_async_remote_copy(
+            src_ref=rsnd.at[n, z], dst_ref=rel.at[n, z], send_sem=ls.at[n, z], recv_sem=lr.at[n, z],
+            device_id={"uly": order(1)}, device_id_type=MESH)
+
     for n in range(parts):
         part = jnp.dot(attended, wo_v[:, n * tile : (n + 1) * tile], preferred_element_type=jnp.float32)
         for z in range(nz):
             own[n, z] = part[z * rows : (z + 1) * rows]
             rsnd[n, z] = part[z * rows : (z + 1) * rows].astype(jnp.bfloat16)
-        for k in range(nz - 1, 0, -1):
-            sum_to(n, order(k)).start()
+        if relayed:
+
+            @pl.when(jnp.logical_not(middle))
+            def _():
+                for k in (3, 2):
+                    relay(n, order(k)).start()
+        else:
+            for k in range(nz - 1, 0, -1):
+                sum_to(n, order(k)).start()
+    if relayed:
+        for n in range(parts):
+            sum_to(n, order(1)).start()
+
+        @pl.when(middle)
+        def _():
+            for n in range(parts):
+                for k in (3, 2):
+                    z = order(k)
+                    relay(n, z).wait_recv()
+                    rsnd[n, z] = (own[n, z] + rel[n, z].astype(jnp.float32)).astype(jnp.bfloat16)
+                    sum_to(n, z).start()
     for n in range(parts):
         total = own[n, mz]
-        for k in range(1, nz):
+        for k in (1, 2) if relayed else range(1, nz):
             z = order(k)
             sum_from(n, z).wait_recv()
             total = total + rrcv[n, z].astype(jnp.float32)
@@ -234,8 +258,21 @@
     for j in range(1, nb):
         back_to(lax.rem(mb + j, nb)).wait_send()
     for n in range(parts):
-        for k in range(1, nz):
+        for k in (1,) if relayed else range(1, nz):
             sum_to(n, order(k)).wait_send()
+    if relayed:
+
+        @pl.when(middle)
+        def _():
+            for n in range(parts):
+                for k in (3, 2):
+                    sum_to(n, order(k)).wait_send()
+
+        @pl.when(jnp.logical_not(middle))
+        def _():
+            for n in range(parts):
+                for k in (3, 2):
+                    relay(n, order(k)).wait_send()
 
 
 def fused(nb, nz, tokens, mod_shift, mod_scale, mod_gate, w_query, w_key, w_value, w_out, score_gain):
@@ -270,6 +307,7 @@
             pltpu.VMEM((parts, nz, rows, tile), f32),
             pltpu.VMEM((parts, nz, rows, tile), bf16),
             pltpu.VMEM((parts, nz, rows, tile), bf16),
+            pltpu.VMEM((parts, nz, rows, tile), bf16),
             dma((9,)),
             dma((nz,)),
             dma((nz,)),
@@ -278,6 +316,8 @@
             dma((nz, nb)),
             dma((nb,)),
             dma((nb,)),
+            dma((parts, nz)),
+            dma((parts, nz)),
             dma((parts, nz)),
             dma((parts, nz)),
         ],

time: 58.4 us -> 58.5 us (level)
  no operation moved by 1% of the time
where the time goes in v3:
time: 58.5 us; the launch traced here: 58.4 us
  Pallas kernels  56.7 us (97%)
  local copies, waits for them, and re-layouts  1.62 us (3%)
    pallas_call x1, Pallas kernels, fused(): pl.pallas_call(functools.partial(kernel, nb, nz), out_shape=jax.ShapeDtyp...  56.7 us
    unnamed x1, local copies, waits for them, and re-layouts  1.62 us

profile of v3, /device:TPU:0, one launch (start us, length us, event | category | flops | bytes accessed | tf_op | source)
XLA Modules:
  0.0 58.4 jit_solution(4648369114280621381)
XLA Ops:
  0.0 56.7 %shard_map.91 = bf16[48,2048]{1,0:T(8,128)(2,1)} custom-call(bf16[48,2048]{1,0:T(8,128)(2,1)} %tok_h.1, f32[1,2048]{1,0:T(1,128)} %bitcast.4, f32[1,2048]{1,0:T(1,128)} %bitcast.5, f32[1,2048]{1,0:T(1,128)} %bitcast.6, f32[1,32]{1,0:T(1,128)} %bitcast.7, bf16[2048,512]{1,0:T(8,128)(2,1)} %wq.1, bf16[2048,512]{1,0:T(8,128)(2,1)} %wk.1, bf16[2048,512]{1,0:T(8,128)(2,1)} %wv.1, ...), custom_call_target="tpu_custom_call" | custom-call | tf_op jit(solution)/shard_map/pallas_call | solution.py:287
  56.7 1.6 %copy.11 = bf16[48,2048]{1,0:T(8,128)(2,1)} copy(bf16[48,2048]{1,0:T(8,128)(2,1)} %shard_map.91) | data formatting | bytes 393216
